TPU v7x, 32 devices: a whole 2x2x4 slice. The times are simulated.
32 devices in a mesh: lon: 8 (over z, x), lat: 4 (over y, core).
Axes of the slice: x: 2, y: 2, z: 4, core: 2. Of those that a mesh axis runs over, the one named last changes fastest.
Arguments:
- inputs: bfloat16 [64, 128, 1024], P(None, 'lon', 'lat'), may hold values from -6 to 6
- weights: bfloat16 [2, 3, 3, 64, 64], replicated, may hold values from -0.25 to 0.25
- biases: float32 [2, 64], replicated, may hold values from -0.5 to 0.5
- cotangent: bfloat16 [64, 128, 1024], P(None, 'lon', 'lat'), may hold values from -6 to 6
Outputs:
- features_out: bfloat16 [64, 128, 1024], P(None, 'lon', 'lat')
- grad_input: bfloat16 [64, 128, 1024], P(None, 'lon', 'lat')
- weight_grads: float32 [2, 3, 3, 64, 64], replicated
- bias_grads: float32 [2, 64], replicated
All inputs are finite; a program needn't handle non-finite values.
Results may differ from a plain program's by a relative error of at most 0.012.
Values may be sent and summed in bfloat16 or wider, within the bound.
No kernel may reach another device: no remote copies, remote signals or barrier semaphores. Data moves between devices by JAX's collectives and lax.ppermute only.
A program may use at most 64 MiB of HBM per device.

v0:
```python
import functools
import math

import jax
import jax.numpy as jnp
import numpy as np
from jax import lax
from jax.experimental import pallas as pl
from jax.experimental.pallas import tpu as pltpu
from jax.sharding import PartitionSpec as P


AXES = ("lon", "lat")
LANES = 128
BF16, F32 = jnp.bfloat16, jnp.float32
PARAMS = pltpu.CompilerParams(vmem_limit_bytes=48 * 2**20)


def lane_order(cols, lat_rows, share):
    steps = lat_rows // cols
    place = np.arange(lat_rows)
    group, rest = place // (steps * share), place % (steps * share)
    source = (rest // share) * cols + group * share + rest % share
    matrix = np.zeros((lat_rows, lat_rows), np.float32)
    matrix[source, place] = 1.0
    return matrix


def pack_kernel(x_ref, cot_ref, order_ref, out_ref, x_buf, cot_buf, rows_ref, sems):
    channels, cols, lat_rows = x_ref.shape
    devices, _, width = out_ref.shape
    groups = devices // cols
    halves = lat_rows // LANES
    copies = [
        pltpu.make_async_copy(ref, buf, sems.at[at])
        for at, (ref, buf) in enumerate(((x_ref, x_buf), (cot_ref, cot_buf)))
    ]
    for copy in copies:
        copy.start()
    for at, buf in enumerate((x_buf, cot_buf)):
        copies[at].wait()
        rows = buf[...].reshape(channels * cols, lat_rows)
        rows = jnp.dot(rows, order_ref[...], preferred_element_type=F32)
        for half in range(halves):
            rows_ref[half] = rows[:, half * LANES : (half + 1) * LANES]
        for col in range(cols):
            column = jnp.concatenate(
                [rows_ref[half, pl.ds(col, channels, stride=cols), :] for half in range(halves)],
                axis=1,
            ).astype(BF16)
            for group in range(groups):
                out_ref[col * groups + group, at * channels : (at + 1) * channels, :] = column[
                    :, group * width : (group + 1) * width
                ]


def unpack_kernel(parts_ref, order_ref, feat_ref, grad_ref, rows_ref):
    channels, cols, lat_rows = feat_ref.shape
    devices, _, width = parts_ref.shape
    groups = devices // cols
    halves = lat_rows // LANES
    for at, out_ref in enumerate((feat_ref, grad_ref)):
        for col in range(cols):
            column = jnp.concatenate(
                [
                    parts_ref[col * groups + g, at * channels : (at + 1) * channels, :]
                    for g in range(groups)
                ],
                axis=1,
            )
            column = jnp.dot(column, order_ref[...], preferred_element_type=F32)
            for half in range(halves):
                rows_ref[half, pl.ds(col, channels, stride=cols), :] = column[
                    :, half * LANES : (half + 1) * LANES
                ]
        for half in range(halves):
            out_ref[:, :, half * LANES : (half + 1) * LANES] = (
                rows_ref[half].astype(BF16).reshape(channels, cols, LANES)
            )


def taps(row, shift):
    edge = jnp.zeros((row.shape[0], shift), row.dtype)
    before = jnp.concatenate([edge, row[:, :-shift]], axis=1)
    after = jnp.concatenate([row[:, shift:], edge], axis=1)
    return before, row, after


def stack_kernel(share, merged, parts_ref, w_ref, b_ref, *refs):
    if merged:
        out_ref, s0_ref, s1_ref, h_ref, y_ref, g_ref, sums_ref = refs
        first = 2 * w_ref.shape[-1]
        pieces_ref = out_ref
    else:
        out_ref, pieces_ref, s0_ref, s1_ref, h_ref, y_ref, g_ref, sums_ref = refs
        first = 0
    count = h_ref.shape[0]
    channels = w_ref.shape[-1]
    devices, _, width = parts_ref.shape
    blocks = devices // count

    def line_of(field, i):
        rows = slice(field * channels, (field + 1) * channels)
        return jnp.concatenate([parts_ref[i * blocks + k, rows, :] for k in range(blocks)], axis=1)

    def put(field, i, line):
        rows = slice(field * channels, (field + 1) * channels)
        for k in range(blocks):
            out_ref[i * blocks + k, rows, :] = line[:, k * width : (k + 1) * width]

    for layer in range(2):
        hops = 2**layer
        kernel = jnp.concatenate(
            [
                jnp.concatenate([w_ref[layer, a, b] for b in range(3)], axis=1)
                for a in range(3)
            ],
            axis=0,
        )
        for i in range(count):
            line = line_of(0, i) if layer == 0 else h_ref[i]
            stack = jnp.concatenate(taps(line, hops * share), axis=0)
            y_ref[i] = jnp.dot(kernel, stack, preferred_element_type=F32)
        bias = b_ref[layer]
        for i in range(count):
            pre = bias + y_ref[i, channels : 2 * channels]
            pre = pre + y_ref[(i - hops) % count, :channels]
            pre = pre + y_ref[(i + hops) % count, 2 * channels :]
            sigma = 1.0 / (1.0 + jnp.exp(-pre))
            state = (pre * sigma).astype(BF16)
            slope = sigma * (1.0 + pre * (1.0 - sigma))
            if layer == 0:
                h_ref[i] = state
                s0_ref[i] = slope
            else:
                s1_ref[i] = slope
                put(0, i, state)

    ones = jnp.ones((16, blocks * width), BF16)
    bias_rows = [None, None]
    for layer in (1, 0):
        hops = 2**layer
        kernel = jnp.concatenate(
            [
                jnp.concatenate([w_ref[layer, a, b].astype(F32).T for b in range(3)], axis=1)
                for a in range(3)
            ],
            axis=0,
        ).astype(BF16)
        total = jnp.zeros((3 * channels, 3 * channels), F32)
        bias = jnp.zeros((16, channels), F32)
        for i in range(count):
            if layer == 1:
                gated = (line_of(1, i).astype(F32) * s1_ref[i]).astype(BF16)
            else:
                gated = g_ref[i]
            bias = bias + lax.dot_general(
                ones, gated, (((1,), (1,)), ((), ())), preferred_element_type=F32
            )
            before, here, after = taps(gated, hops * share)
            stack = jnp.concatenate([after, here, before], axis=0)
            y_ref[i] = jnp.dot(kernel, stack, preferred_element_type=F32)
            around = [(i + (a - 1) * hops) % count for a in range(3)]
            lines = jnp.concatenate(
                [line_of(0, j) if layer == 0 else h_ref[j] for j in around], axis=0
            )
            total = total + lax.dot_general(
                stack, lines, (((1,), (1,)), ((), ())), preferred_element_type=F32
            )
        high = 3 * channels
        sums_ref[layer * high : (layer + 1) * high, :] = total[:, : 2 * channels]
        sums_ref[2 * high : 3 * high, layer * channels : (layer + 1) * channels] = total[
            :, 2 * channels :
        ]
        bias_rows[layer] = bias[:1]
        for i in range(count):
            g = y_ref[i, channels : 2 * channels]
            g = g + y_ref[(i + hops) % count, :channels]
            g = g + y_ref[(i - hops) % count, 2 * channels :]
            g = g.astype(BF16)
            if layer == 1:
                g_ref[i] = (g.astype(F32) * s0_ref[i]).astype(BF16)
            else:
                put(1, i, g)

    used = -(-9 * channels // devices)
    held = sums_ref.shape[0] - 9 * channels
    sums_ref[9 * channels :, :] = jnp.zeros((held, 2 * channels), F32)
    size = pieces_ref.shape[1] - first
    bias = jnp.concatenate(bias_rows, axis=1)
    high = bias.astype(BF16).astype(F32)
    low = bias - high
    row = lax.broadcasted_iota(jnp.int32, (size, 2 * channels), 0)
    for p in range(devices):
        piece = sums_ref[used * p : used * p + size, :]
        piece = jnp.where(row < used, piece, jnp.where(row == used, high, low))
        pieces_ref[p, first:, :] = piece.astype(BF16)


def reduce_kernel(scale, used, first, got_ref, mine_ref, bias_ref):
    devices, size, lanes = mine_ref.shape
    total = got_ref[0, first:, :].astype(F32)
    for p in range(1, devices):
        total = total + got_ref[p, first:, :].astype(F32)
    total = total * scale
    bias = total[used : used + 1] + total[used + 1 : used + 2]
    bias_ref[0:1, :] = bias[:, : lanes // 2]
    bias_ref[1:2, :] = bias[:, lanes // 2 :]
    total = total.astype(BF16)
    for p in range(devices):
        mine_ref[p] = total


def assemble_kernel(used, parts_ref, out_ref, rows_ref):
    devices = parts_ref.shape[0]
    channels = out_ref.shape[-1]
    for p in range(devices):
        rows_ref[used * p : used * (p + 1), :] = parts_ref[p].astype(F32)[:used]
    high = 3 * channels
    for layer in range(2):
        for b in range(3):
            pair = rows_ref[layer * high + b * channels : layer * high + (b + 1) * channels, :]
            out_ref[layer, 0, b] = pair[:, :channels]
            out_ref[layer, 1, b] = pair[:, channels:]
            third = rows_ref[2 * high + b * channels : 2 * high + (b + 1) * channels, :]
            out_ref[layer, 2, b] = third[:, layer * channels : (layer + 1) * channels]


def exchanged(parts):
    return lax.all_to_all(parts, AXES, 0, 0, tiled=True)


def local(inputs, weights, biases, cotangent):
    channels, cols, lat_rows = inputs.shape
    lons, lats = lax.axis_size("lon"), lax.axis_size("lat")
    devices = lons * lats
    share = cols * cols // devices
    width = lat_rows // cols * share
    span = lats * width
    scale = 1.0 / math.sqrt(cols * lons * lat_rows * lats)
    order = lane_order(cols, lat_rows, share)
    into = jnp.asarray(order, BF16)
    back = jnp.asarray(order.T, BF16)
    merged = width == LANES
    used = -(-9 * channels // devices)
    size = -(-(used + 2) // 8) * 8
    shape = jax.ShapeDtypeStruct
    rows = pltpu.VMEM((lat_rows // LANES, channels * cols, LANES), F32)

    packed = pl.pallas_call(
        pack_kernel,
        out_shape=shape((devices, 2 * channels, width), BF16),
        in_specs=[
            pl.BlockSpec(memory_space=pl.ANY),
            pl.BlockSpec(memory_space=pl.ANY),
            pl.BlockSpec(memory_space=pltpu.VMEM),
        ],
        scratch_shapes=[
            pltpu.VMEM(inputs.shape, BF16),
            pltpu.VMEM(inputs.shape, BF16),
            rows,
            pltpu.SemaphoreType.DMA((2,)),
        ],
        compiler_params=PARAMS,
    )(inputs, cotangent, into)
    parts = exchanged(packed)
    if not merged:
        parts = parts.reshape(lons, lats, 2 * channels, width).transpose(0, 2, 1, 3)
        parts = parts.reshape(lons, 2 * channels, span)

    cells = (lons, channels, span)
    pieces_shape = (devices, size, 2 * channels)
    if merged:
        out_shape = [shape((devices, 2 * channels + size, width), BF16)]
    else:
        out_shape = [shape(parts.shape, BF16), shape(pieces_shape, BF16)]
    results = pl.pallas_call(
        functools.partial(stack_kernel, share, merged),
        out_shape=out_shape,
        scratch_shapes=[
            pltpu.VMEM(cells, F32),
            pltpu.VMEM(cells, F32),
            pltpu.VMEM(cells, BF16),
            pltpu.VMEM((lons, 3 * channels, span), F32),
            pltpu.VMEM(cells, BF16),
            pltpu.VMEM((used * devices + size, 2 * channels), F32),
        ],
        compiler_params=PARAMS,
    )(parts, weights, biases[:, :, None])
    if merged:
        home = exchanged(results[0])
        got, first = home, 2 * channels
    else:
        home = results[0].reshape(lons, 2 * channels, lats, width).transpose(0, 2, 1, 3)
        home = exchanged(home.reshape(devices, 2 * channels, width))
        got, first = exchanged(results[1]), 0

    mine, bias_grads = pl.pallas_call(
        functools.partial(reduce_kernel, scale, used, first),
        out_shape=[shape(pieces_shape, BF16), shape(biases.shape, F32)],
        compiler_params=PARAMS,
    )(got)
    home, mine = lax.optimization_barrier((home, mine))
    full = exchanged(mine)
    features_out, grad_input = pl.pallas_call(
        unpack_kernel,
        out_shape=[shape(inputs.shape, BF16), shape(inputs.shape, BF16)],
        scratch_shapes=[rows],
        compiler_params=PARAMS,
        cost_estimate=pl.CostEstimate(
            flops=4 * inputs.size * lat_rows, bytes_accessed=8 * inputs.size, transcendentals=0
        ),
    )(home, back)
    weight_grads = pl.pallas_call(
        functools.partial(assemble_kernel, used),
        out_shape=shape(weights.shape, F32),
        scratch_shapes=[pltpu.VMEM((used * devices, 2 * channels), F32)],
        compiler_params=PARAMS,
    )(full)
    return features_out, grad_input, weight_grads, bias_grads


def solution(mesh):
    in_specs = (P(None, "lon", "lat"), P(), P(), P(None, "lon", "lat"))
    out_specs = (P(None, "lon", "lat"), P(None, "lon", "lat"), P(), P())
    return jax.shard_map(local, mesh=mesh, in_specs=in_specs, out_specs=out_specs, check_vma=False)
```

profile of v0, /device:TPU:0, one launch (start us, length us, event | category | flops | bytes accessed | tf_op | source)
XLA Modules:
  0.0 93.6 jit_solution(7103359342279467425)
XLA Ops:
  0.6 0.0 copy-start
  0.6 1.0 %copy-done = bf16[64,16,256]{2,1,0:T(8,128)(2,1)S(1)} copy-done((bf16[64,16,256]{2,1,0:T(8,128)(2,1)S(1)}, bf16[64,16,256]{2,1,0:T(8,128)(2,1)}, u32[]{:S(2)}) %copy-start) | copy-done | bytes 524312
  1.7 0.0 copy-start.1
  1.7 1.0 %copy-done.1 = bf16[64,16,256]{2,1,0:T(8,128)(2,1)S(1)} copy-done((bf16[64,16,256]{2,1,0:T(8,128)(2,1)S(1)}, bf16[64,16,256]{2,1,0:T(8,128)(2,1)}, u32[]{:S(2)}) %copy-start.1) | copy-done | bytes 524312
  2.7 0.0 copy-start.3
  2.7 0.9 copy-done.3
  3.6 2.3 %shard_map.93 = bf16[32,128,128]{2,1,0:T(8,128)(2,1)} custom-call(bf16[64,16,256]{2,1,0:T(8,128)(2,1)S(1)} %copy-done, bf16[64,16,256]{2,1,0:T(8,128)(2,1)S(1)} %copy-done.1, bf16[256,256]{1,0:T(8,128)(2,1)S(1)} %copy-done.3), custom_call_target="tpu_custom_call" | custom-call | tf_op jit(solution)/shard_map/pallas_call | solution.py:250
  5.9 0.0 copy-start.5
  6.0 0.0 copy-start.2
  6.0 7.3 %all-to-all-start = ((bf16[32,128,128]{2,1,0:T(8,128)(2,1)}), bf16[32,128,128]{2,1,0:T(8,128)(2,1)S(1)}, u32[]{:S(2)}, u32[]{:S(2)}) async-start(bf16[32,128,128]{2,1,0:T(8,128)(2,1)} %shard_map.93), calls=%async_computation | async-start | bytes 2097152 | tf_op jit(solution)/shard_map/all_to_all | solution.py:230
  13.3 0.0 copy-done.5
  13.3 0.1 copy.10.b_ref
  13.4 26.1 %all-to-all-done.parts_ref = bf16[32,128,128]{2,1,0:T(8,128)(2,1)S(1)} async-done(((bf16[32,128,128]{2,1,0:T(8,128)(2,1)}), bf16[32,128,128]{2,1,0:T(8,128)(2,1)S(1)}, u32[]{:S(2)}, u32[]{:S(2)}) %all-to-all-start) | async-done | bytes 1048608 | tf_op jit(solution)/shard_map/all_to_all | solution.py:230
  39.5 0.0 copy-done.2
  39.5 5.6 %shard_map.94 = bf16[32,152,128]{2,1,0:T(8,128)(2,1)S(1)} custom-call(bf16[32,128,128]{2,1,0:T(8,128)(2,1)S(1)} %all-to-all-done.parts_ref, bf16[2,3,3,64,64]{4,3,2,1,0:T(8,128)(2,1)S(1)} %copy-done.2, f32[2,64,1]{2,1,0:T(8,128)S(1)} %copy.10.b_ref), custom_call_target="tpu_custom_call" | custom-call | tf_op jit(solution)/shard_map/pallas_call | solution.py:277
  45.1 35.4 %all_to_all.15.got_ref.parts_ref = bf16[32,152,128]{2,1,0:T(8,128)(2,1)S(1)} all-to-all(bf16[32,152,128]{2,1,0:T(8,128)(2,1)S(1)} %shard_map.94), channel_id=1, replica_groups=mesh['lon'=8,'lat'=4] {'lon','lat'}, dimensions={0} | all-to-all | bytes 2490368 | tf_op jit(solution)/shard_map/all_to_all | solution.py:230
  80.5 0.0 copy-start.4
  80.5 0.7 shard_map.95
  81.2 2.6 %all-to-all-start.2 = ((bf16[32,24,128]{2,1,0:T(8,128)(2,1)}), bf16[32,24,128]{2,1,0:T(8,128)(2,1)S(1)}, u32[]{:S(2)}, u32[]{:S(2)}) async-start(bf16[32,24,128]{2,1,0:T(8,128)(2,1)} %get-tuple-element.14), calls=%async_computation.2 | async-start | bytes 393216 | tf_op jit(solution)/shard_map/all_to_all | solution.py:230
  83.8 0.0 copy-done.4
  83.8 2.0 %shard_map.96 = (bf16[64,16,256]{2,1,0:T(8,128)(2,1)}, bf16[64,16,256]{2,1,0:T(8,128)(2,1)}) custom-call(bf16[32,152,128]{2,1,0:T(8,128)(2,1)S(1)} %all_to_all.15.got_ref.parts_ref, bf16[256,256]{1,0:T(8,128)(2,1)S(1)} %copy-done.4), custom_call_target="tpu_custom_call" | custom-call | flops 268435456 | bytes 2097152 | tf_op jit(solution)/shard_map/pallas_call | solution.py:305
  85.8 6.9 %all-to-all-done.2.parts_ref = bf16[32,24,128]{2,1,0:T(8,128)(2,1)S(1)} async-done(((bf16[32,24,128]{2,1,0:T(8,128)(2,1)}), bf16[32,24,128]{2,1,0:T(8,128)(2,1)S(1)}, u32[]{:S(2)}, u32[]{:S(2)}) %all-to-all-start.2) | async-done | bytes 196640 | tf_op jit(solution)/shard_map/all_to_all | solution.py:230
  92.7 1.0 %shard_map.97 = f32[2,3,3,64,64]{4,3,2,1,0:T(8,128)} custom-call(bf16[32,24,128]{2,1,0:T(8,128)(2,1)S(1)} %all-to-all-done.2.parts_ref), custom_call_target="tpu_custom_call" | custom-call | tf_op jit(solution)/shard_map/pallas_call | solution.py:314
Async XLA Ops:
  0.6 1.0 %copy-start = (bf16[64,16,256]{2,1,0:T(8,128)(2,1)S(1)}, bf16[64,16,256]{2,1,0:T(8,128)(2,1)}, u32[]{:S(2)}) copy-start(bf16[64,16,256]{2,1,0:T(8,128)(2,1)} %x_ref.1) | copy-start | bytes 1572868
  1.7 1.0 %copy-start.1 = (bf16[64,16,256]{2,1,0:T(8,128)(2,1)S(1)}, bf16[64,16,256]{2,1,0:T(8,128)(2,1)}, u32[]{:S(2)}) copy-start(bf16[64,16,256]{2,1,0:T(8,128)(2,1)} %cot_ref.1) | copy-start | bytes 1572868
  2.7 0.9 copy-start.3
  5.9 7.3 %copy-start.5 = (f32[2,64]{1,0:T(2,128)S(1)}, f32[2,64]{1,0:T(2,128)}, u32[]{:S(2)}) copy-start(f32[2,64]{1,0:T(2,128)} %param.8) | copy-start | bytes 1540
  6.0 33.6 %copy-start.2 = (bf16[2,3,3,64,64]{4,3,2,1,0:T(8,128)(2,1)S(1)}, bf16[2,3,3,64,64]{4,3,2,1,0:T(8,128)(2,1)}, u32[]{:S(2)}) copy-start(bf16[2,3,3,64,64]{4,3,2,1,0:T(8,128)(2,1)} %w_ref.1) | copy-start | bytes 442372
  6.0 33.5 %all-to-all-start = ((bf16[32,128,128]{2,1,0:T(8,128)(2,1)}), bf16[32,128,128]{2,1,0:T(8,128)(2,1)S(1)}, u32[]{:S(2)}, u32[]{:S(2)}) async-start(bf16[32,128,128]{2,1,0:T(8,128)(2,1)} %shard_map.93), calls=%async_computation | async-start | bytes 2097152 | tf_op jit(solution)/shard_map/all_to_all | solution.py:230
  80.5 3.3 %copy-start.4 = (bf16[256,256]{1,0:T(8,128)(2,1)S(1)}, bf16[256,256]{1,0:T(8,128)(2,1)}, u32[]{:S(2)}) copy-start(bf16[256,256]{1,0:T(8,128)(2,1)} %constant.5.clone.order_ref) | copy-start | bytes 393220
  81.2 11.5 %all-to-all-start.2 = ((bf16[32,24,128]{2,1,0:T(8,128)(2,1)}), bf16[32,24,128]{2,1,0:T(8,128)(2,1)S(1)}, u32[]{:S(2)}, u32[]{:S(2)}) async-start(bf16[32,24,128]{2,1,0:T(8,128)(2,1)} %get-tuple-element.14), calls=%async_computation.2 | async-start | bytes 393216 | tf_op jit(solution)/shard_map/all_to_all | solution.py:230
where the time goes:
time: 94.2 us; the launch traced here: 93.6 us
  blocking collectives  35.4 us (38%)
  waiting for transfers between devices  33 us (35%)
  Pallas kernels  11.5 us (12%)
  starting transfers between devices  9.88 us (10%)
  local copies, waits for them, and re-layouts  3.1 us (3%)
    all_to_all x1, blocking collectives, exchanged(): return lax.all_to_all(parts, AXES, 0, 0, tiled=True)  35.4 us
    all_to_all x2, waiting for transfers between devices, exchanged(): return lax.all_to_all(parts, AXES, 0, 0, tiled=True)  33 us
    all_to_all x2, starting transfers between devices, exchanged(): return lax.all_to_all(parts, AXES, 0, 0, tiled=True)  9.88 us
    pallas_call x1, Pallas kernels, local(): pl.pallas_call(functools.partial(stack_kernel, share, merged), out_shape=...  5.56 us
    unnamed x12, local copies, waits for them, and re-layouts  3 us
    pallas_call x1, Pallas kernels, local(): pl.pallas_call(pack_kernel, out_shape=shape((devices, 2 * channels, width...  2.32 us
    pallas_call x1, Pallas kernels, local(): pl.pallas_call(unpack_kernel, out_shape=[shape(inputs.shape, BF16), shape...  1.99 us
  transfers between devices with their start and end apart: 2, of which 2 were waited for; matrix products, arithmetic and copies ran while one was open for 0% of the time, Pallas kernels for 2%

commit v1 on v0

--- a/solution.py
+++ b/solution.py
@@ -3,7 +3,6 @@
 
 import jax
 import jax.numpy as jnp
-import numpy as np
 from jax import lax
 from jax.experimental import pallas as pl
 from jax.experimental.pallas import tpu as pltpu
@@ -16,17 +15,16 @@
 PARAMS = pltpu.CompilerParams(vmem_limit_bytes=48 * 2**20)
 
 
-def lane_order(cols, lat_rows, share):
+def lane_order(cols, lat_rows, share, inverse):
     steps = lat_rows // cols
-    place = np.arange(lat_rows)
-    group, rest = place // (steps * share), place % (steps * share)
-    source = (rest // share) * cols + group * share + rest % share
-    matrix = np.zeros((lat_rows, lat_rows), np.float32)
-    matrix[source, place] = 1.0
-    return matrix
-
-
-def pack_kernel(x_ref, cot_ref, order_ref, out_ref, x_buf, cot_buf, rows_ref, sems):
+    place = lax.broadcasted_iota(jnp.int32, (lat_rows, lat_rows), 0 if inverse else 1)
+    source = lax.broadcasted_iota(jnp.int32, (lat_rows, lat_rows), 1 if inverse else 0)
+    group = lax.div(source & (cols - 1), share)
+    wanted = (group * steps + lax.div(source, cols)) * share + (source & (share - 1))
+    return (place == wanted).astype(F32).astype(BF16)
+
+
+def pack_kernel(share, x_ref, cot_ref, out_ref, x_buf, cot_buf, rows_ref, sems):
     channels, cols, lat_rows = x_ref.shape
     devices, _, width = out_ref.shape
     groups = devices // cols
@@ -37,10 +35,11 @@
     ]
     for copy in copies:
         copy.start()
+    order = lane_order(cols, lat_rows, share, False)
     for at, buf in enumerate((x_buf, cot_buf)):
         copies[at].wait()
         rows = buf[...].reshape(channels * cols, lat_rows)
-        rows = jnp.dot(rows, order_ref[...], preferred_element_type=F32)
+        rows = jnp.dot(rows, order, preferred_element_type=F32)
         for half in range(halves):
             rows_ref[half] = rows[:, half * LANES : (half + 1) * LANES]
         for col in range(cols):
@@ -54,11 +53,12 @@
                 ]
 
 
-def unpack_kernel(parts_ref, order_ref, feat_ref, grad_ref, rows_ref):
+def unpack_kernel(share, parts_ref, feat_ref, grad_ref, rows_ref):
     channels, cols, lat_rows = feat_ref.shape
     devices, _, width = parts_ref.shape
     groups = devices // cols
     halves = lat_rows // LANES
+    order = lane_order(cols, lat_rows, share, True)
     for at, out_ref in enumerate((feat_ref, grad_ref)):
         for col in range(cols):
             column = jnp.concatenate(
@@ -68,7 +68,7 @@
                 ],
                 axis=1,
             )
-            column = jnp.dot(column, order_ref[...], preferred_element_type=F32)
+            column = jnp.dot(column, order, preferred_element_type=F32)
             for half in range(halves):
                 rows_ref[half, pl.ds(col, channels, stride=cols), :] = column[
                     :, half * LANES : (half + 1) * LANES
@@ -198,7 +198,7 @@
 
 
 def reduce_kernel(scale, used, first, got_ref, mine_ref, bias_ref):
-    devices, size, lanes = mine_ref.shape
+    devices, lanes = got_ref.shape[0], mine_ref.shape[1]
     total = got_ref[0, first:, :].astype(F32)
     for p in range(1, devices):
         total = total + got_ref[p, first:, :].astype(F32)
@@ -206,9 +206,7 @@
     bias = total[used : used + 1] + total[used + 1 : used + 2]
     bias_ref[0:1, :] = bias[:, : lanes // 2]
     bias_ref[1:2, :] = bias[:, lanes // 2 :]
-    total = total.astype(BF16)
-    for p in range(devices):
-        mine_ref[p] = total
+    mine_ref[...] = total.astype(BF16)
 
 
 def assemble_kernel(used, parts_ref, out_ref, rows_ref):
@@ -238,9 +236,6 @@
     width = lat_rows // cols * share
     span = lats * width
     scale = 1.0 / math.sqrt(cols * lons * lat_rows * lats)
-    order = lane_order(cols, lat_rows, share)
-    into = jnp.asarray(order, BF16)
-    back = jnp.asarray(order.T, BF16)
     merged = width == LANES
     used = -(-9 * channels // devices)
     size = -(-(used + 2) // 8) * 8
@@ -248,12 +243,11 @@
     rows = pltpu.VMEM((lat_rows // LANES, channels * cols, LANES), F32)
 
     packed = pl.pallas_call(
-        pack_kernel,
+        functools.partial(pack_kernel, share),
         out_shape=shape((devices, 2 * channels, width), BF16),
         in_specs=[
-            pl.BlockSpec(memory_space=pl.ANY),
-            pl.BlockSpec(memory_space=pl.ANY),
-            pl.BlockSpec(memory_space=pltpu.VMEM),
+            pl.BlockSpec(memory_space=pltpu.HBM),
+            pl.BlockSpec(memory_space=pltpu.HBM),
         ],
         scratch_shapes=[
             pltpu.VMEM(inputs.shape, BF16),
@@ -261,8 +255,8 @@
             rows,
             pltpu.SemaphoreType.DMA((2,)),
         ],
-        compiler_params=PARAMS,
-    )(inputs, cotangent, into)
+        compiler_params=pltpu.CompilerParams(vmem_limit_bytes=56 * 2**20),
+    )(inputs, cotangent)
     parts = exchanged(packed)
     if not merged:
         parts = parts.reshape(lons, lats, 2 * channels, width).transpose(0, 2, 1, 3)
@@ -297,20 +291,20 @@
 
     mine, bias_grads = pl.pallas_call(
         functools.partial(reduce_kernel, scale, used, first),
-        out_shape=[shape(pieces_shape, BF16), shape(biases.shape, F32)],
+        out_shape=[shape(pieces_shape[1:], BF16), shape(biases.shape, F32)],
         compiler_params=PARAMS,
     )(got)
     home, mine = lax.optimization_barrier((home, mine))
-    full = exchanged(mine)
+    full = lax.all_gather(mine, AXES)
     features_out, grad_input = pl.pallas_call(
-        unpack_kernel,
+        functools.partial(unpack_kernel, share),
         out_shape=[shape(inputs.shape, BF16), shape(inputs.shape, BF16)],
         scratch_shapes=[rows],
         compiler_params=PARAMS,
         cost_estimate=pl.CostEstimate(
             flops=4 * inputs.size * lat_rows, bytes_accessed=8 * inputs.size, transcendentals=0
         ),
-    )(home, back)
+    )(home)
     weight_grads = pl.pallas_call(
         functools.partial(assemble_kernel, used),
         out_shape=shape(weights.shape, F32),

time: 94.2 us -> 121 us (1.28)
  blocking collectives: 35.4 us -> 73.9 us
  waiting for transfers between devices: 33 us -> 26.1 us
  local copies, waits for them, and re-layouts: 3.1 us -> 0.11 us
  starting transfers between devices: 9.88 us -> 7.3 us
    all_gather x0 -> x1, blocking collectives: none -> 38.6 us  [local(): full = lax.all_gather(mine, AXES)]
    all_to_all x2 -> x1, waiting for transfers between devices: 33 us -> 26.1 us  [exchanged(): return lax.all_to_all(parts, AXES, 0, 0, tiled=True)]
    unnamed x12 -> x4, local copies, waits for them, and re-layouts: 3 us -> 0.01 us
    all_to_all x2 -> x1, starting transfers between devices: 9.88 us -> 7.3 us  [exchanged(): return lax.all_to_all(parts, AXES, 0, 0, tiled=True)]
  transfers between devices with their start and end apart: 2 -> 1, of which waited for: 2 -> 1; matrix products, arithmetic and copies ran while one was open for 0% -> 0% of each run, Pallas kernels for 2% -> 0%
where the time goes in v1:
time: 121 us
  blocking collectives  73.9 us (61%)
  waiting for transfers between devices  26.1 us (22%)
  Pallas kernels  12.4 us (10%)
  starting transfers between devices  7.3 us (6%)
    all_gather x1, blocking collectives, local(): full = lax.all_gather(mine, AXES)  38.6 us
    all_to_all x1, blocking collectives, exchanged(): return lax.all_to_all(parts, AXES, 0, 0, tiled=True)  35.4 us
    all_to_all x1, waiting for transfers between devices, exchanged(): return lax.all_to_all(parts, AXES, 0, 0, tiled=True)  26.1 us
    all_to_all x1, starting transfers between devices, exchanged(): return lax.all_to_all(parts, AXES, 0, 0, tiled=True)  7.3 us
    pallas_call x1, Pallas kernels, local(): pl.pallas_call(functools.partial(stack_kernel, share, merged), out_shape=...  5.56 us
    pallas_call x1, Pallas kernels, local(): pl.pallas_call(functools.partial(pack_kernel, share), out_shape=shape((de...  3.28 us
  transfers between devices with their start and end apart: 1, of which 1 were waited for; matrix products, arithmetic and copies ran while one was open for 0% of the time, Pallas kernels for 0%

profile of v1, /device:TPU:0, one launch (start us, length us, event | category | flops | bytes accessed | tf_op | source)
XLA Modules:
  0.0 120.6 jit_solution(835775467668123674)
XLA Ops:
  0.6 3.3 %shard_map.75 = bf16[32,128,128]{2,1,0:T(8,128)(2,1)} custom-call(bf16[64,16,256]{2,1,0:T(8,128)(2,1)} %x_ref.1, bf16[64,16,256]{2,1,0:T(8,128)(2,1)} %cot_ref.1), custom_call_target="tpu_custom_call" | custom-call | tf_op jit(solution)/shard_map/pallas_call | solution.py:245
  3.9 0.0 copy-start.1
  3.9 0.0 copy-start
  3.9 7.3 %all-to-all-start = ((bf16[32,128,128]{2,1,0:T(8,128)(2,1)}), bf16[32,128,128]{2,1,0:T(8,128)(2,1)S(1)}, u32[]{:S(2)}, u32[]{:S(2)}) async-start(bf16[32,128,128]{2,1,0:T(8,128)(2,1)} %shard_map.75), calls=%async_computation | async-start | bytes 2097152 | tf_op jit(solution)/shard_map/all_to_all | solution.py:228
  11.3 0.0 copy-done.1
  11.3 0.1 copy.8.b_ref
  11.4 26.1 %all-to-all-done.parts_ref = bf16[32,128,128]{2,1,0:T(8,128)(2,1)S(1)} async-done(((bf16[32,128,128]{2,1,0:T(8,128)(2,1)}), bf16[32,128,128]{2,1,0:T(8,128)(2,1)S(1)}, u32[]{:S(2)}, u32[]{:S(2)}) %all-to-all-start) | async-done | bytes 1048608 | tf_op jit(solution)/shard_map/all_to_all | solution.py:228
  37.5 0.0 copy-done
  37.5 5.6 %shard_map.76 = bf16[32,152,128]{2,1,0:T(8,128)(2,1)S(1)} custom-call(bf16[32,128,128]{2,1,0:T(8,128)(2,1)S(1)} %all-to-all-done.parts_ref, bf16[2,3,3,64,64]{4,3,2,1,0:T(8,128)(2,1)S(1)} %copy-done, f32[2,64,1]{2,1,0:T(8,128)S(1)} %copy.8.b_ref), custom_call_target="tpu_custom_call" | custom-call | tf_op jit(solution)/shard_map/pallas_call | solution.py:271
  43.1 35.4 %all_to_all.10.got_ref.parts_ref = bf16[32,152,128]{2,1,0:T(8,128)(2,1)S(1)} all-to-all(bf16[32,152,128]{2,1,0:T(8,128)(2,1)S(1)} %shard_map.76), channel_id=1, replica_groups=mesh['lon'=8,'lat'=4] {'lon','lat'}, dimensions={0} | all-to-all | bytes 2490368 | tf_op jit(solution)/shard_map/all_to_all | solution.py:228
  78.4 0.7 shard_map.77
  79.1 2.0 %shard_map.78 = (bf16[64,16,256]{2,1,0:T(8,128)(2,1)}, bf16[64,16,256]{2,1,0:T(8,128)(2,1)}) custom-call(bf16[32,152,128]{2,1,0:T(8,128)(2,1)S(1)} %all_to_all.10.got_ref.parts_ref), custom_call_target="tpu_custom_call" | custom-call | flops 268435456 | bytes 2097152 | tf_op jit(solution)/shard_map/pallas_call | solution.py:299
  81.1 38.6 %all-gather = bf16[768,128]{1,0:T(8,128)(2,1)S(1)} all-gather(bf16[24,128]{1,0:T(8,128)(2,1)S(1)} %get-tuple-element.14), channel_id=2, replica_groups=mesh['lon'=8,'lat'=4] {'lon','lat'}, dimensions={0}, use_global_device_ids=true | all-gather | bytes 202752 | tf_op jit(solution)/shard_map/all_gather | solution.py:298
  119.6 1.0 shard_map.79
Async XLA Ops:
  3.9 7.3 %copy-start.1 = (f32[2,64]{1,0:T(2,128)S(1)}, f32[2,64]{1,0:T(2,128)}, u32[]{:S(2)}) copy-start(f32[2,64]{1,0:T(2,128)} %param.6) | copy-start | bytes 1540
  3.9 33.6 %copy-start = (bf16[2,3,3,64,64]{4,3,2,1,0:T(8,128)(2,1)S(1)}, bf16[2,3,3,64,64]{4,3,2,1,0:T(8,128)(2,1)}, u32[]{:S(2)}) copy-start(bf16[2,3,3,64,64]{4,3,2,1,0:T(8,128)(2,1)} %w_ref.1) | copy-start | bytes 442372
  3.9 33.5 %all-to-all-start = ((bf16[32,128,128]{2,1,0:T(8,128)(2,1)}), bf16[32,128,128]{2,1,0:T(8,128)(2,1)S(1)}, u32[]{:S(2)}, u32[]{:S(2)}) async-start(bf16[32,128,128]{2,1,0:T(8,128)(2,1)} %shard_map.75), calls=%async_computation | async-start | bytes 2097152 | tf_op jit(solution)/shard_map/all_to_all | solution.py:228
